TPU v7x, 32 devices: a whole 2x2x4 slice. The times are simulated.
32 devices in a mesh: lat: 4 (over y, core), lon: 8 (over z, x).
Axes of the slice: x: 2, y: 2, z: 4, core: 2. Of those that a mesh axis runs over, the one named last changes fastest.
Arguments:
- latent: bfloat16 [64, 768, 256], P('lat', 'lon'), may hold values from -6 to 6
- ocean_mask: int32 [64, 768], P('lat', 'lon'), may hold values from 0 to 1, as said below
- depth_kernel: bfloat16 [7, 7, 256], replicated, may hold values from -0.875 to 0.875
- expand_weight: bfloat16 [256, 1024], replicated, may hold values from -0.375 to 0.375
- reduce_weight: bfloat16 [1024, 256], replicated, may hold values from -0.1875 to 0.1875
- decode_weight: bfloat16 [256, 304], replicated, may hold values from -0.375 to 0.375
- column_in: bfloat16 [304, 1024], replicated, may hold values from -0.3125 to 0.3125
- column_out: bfloat16 [1024, 304], replicated, may hold values from -0.1875 to 0.1875
- state_cot: bfloat16 [64, 768, 304], P('lat', 'lon'), may hold values from -6 to 6
Outputs:
- state: bfloat16 [64, 768, 304], P('lat', 'lon')
- grad_latent: bfloat16 [64, 768, 256], P('lat', 'lon')
- grad_kernel: float32 [7, 7, 256], P(None, None, ('lat', 'lon'))
- grad_expand: float32 [256, 1024], P(None, ('lat', 'lon'))
- grad_reduce: float32 [1024, 256], P(('lat', 'lon'))
- grad_decode: float32 [256, 304], P(('lat', 'lon'))
- grad_column_in: float32 [304, 1024], P(None, ('lat', 'lon'))
- grad_column_out: float32 [1024, 304], P(('lat', 'lon'))
Inputs may be any that keep to these rules, and one draw needn't show every extreme that they name: `ocean_mask`: exactly 18432 cells are ocean (1), the rest land (0); at least one device's tile is all ocean.
All inputs are finite; a program needn't handle non-finite values.
Results may differ from a plain program's by a relative error of at most 0.008.
Values may be sent and summed in bfloat16 or wider, within the bound.
A program may use at most 128 MiB of HBM per device.

v0:
```python
import functools
import math

import jax
import jax.numpy as jnp
from jax import lax
from jax.experimental import pallas as pl
from jax.experimental.pallas import tpu as pltpu
from jax.sharding import PartitionSpec as P

KERNEL = 7


EPSILON = 1e-06


MESH = pl.DeviceIdType.MESH
SIDE = 8


def barrier_with(peers):
    barrier = pltpu.get_barrier_semaphore()
    for peer in peers:
        pl.semaphore_signal(barrier, inc=1, device_id=peer, device_id_type=MESH)
    pl.semaphore_wait(barrier, len(peers))


def sender(send_sem, recv_sem):
    slots = iter(range(send_sem.shape[0]))

    def send(src, dst, peer):
        at = next(slots)
        copy = pltpu.make_async_remote_copy(
            src_ref=src,
            dst_ref=dst,
            send_sem=send_sem.at[at],
            recv_sem=recv_sem.at[at],
            device_id=peer,
            device_id_type=MESH,
        )
        copy.start()
        return copy

    return send


WAYS = [(i, j) for i in (0, 1, -1) for j in (0, 1, -1) if (i, j) != (0, 0)]


def rim_peers(lat_count, lon_count):
    lat, lon = lax.axis_index("lat"), lax.axis_index("lon")
    return [
        (lax.rem(lat + i + lat_count, lat_count), lax.rem(lon + j + lon_count, lon_count))
        for i, j in WAYS
    ]


def send_rim(send, peers, radius, x_ref, edge_ref, got_rows, got_edges):
    rows = x_ref.shape[0]
    copies = []
    for (i, j), peer in zip(WAYS, peers):
        if j == 0:
            first, slot = (rows - radius, 0) if i == 1 else (0, 1)
            copies.append(send(x_ref.at[pl.ds(first, radius)], got_rows.at[slot], peer))
        else:
            side = 1 if j == 1 else 0
            copies.append(send(edge_ref.at[side], got_edges.at[1 - side, i + 1], peer))
    return copies


def fill_tile(radius, x_ref, wide):
    rows, cols, channels = x_ref.shape
    for at in (0, SIDE + cols):
        wide[:, at : at + SIDE] = jnp.zeros((wide.shape[0], SIDE, channels), wide.dtype)

    @pl.loop(0, rows)
    def _(row):
        wide[row + radius, SIDE : SIDE + cols] = x_ref[row].astype(jnp.float32)


def fill_rim(lat_count, radius, x_ref, wide, got_rows, got_edges):
    rows, cols, channels = x_ref.shape
    lat = lax.axis_index("lat")
    for slot, low in ((0, 0), (1, rows + radius)):
        for r in range(radius):
            wide[low + r, SIDE : SIDE + cols] = got_rows[slot, r].astype(jnp.float32)
    for side, left in ((0, SIDE - radius), (1, SIDE + cols)):
        for i, first, low, count in (
            (0, 0, radius, rows),
            (1, rows - radius, 0, radius),
            (-1, 0, rows + radius, radius),
        ):
            for col in range(radius):
                block = got_edges[side, i + 1, col].astype(jnp.float32)
                for r in range(count):
                    wide[low + r, left + col : left + col + 1] = block[first + r : first + r + 1]
    for edge, low in ((0, 0), (lat_count - 1, rows + radius)):

        @pl.when(lat == edge)
        def _():
            wide[low : low + radius] = jnp.zeros((radius,) + wide.shape[1:], wide.dtype)


def conv_rows(wide, taps_ref, out_ref, low, high):
    cols, channels = out_ref.shape[1:]
    width = wide.shape[1]

    @pl.loop(low, high)
    def _(row):
        for lane in range(0, channels, 128):
            lanes = slice(lane, lane + 128)
            total = None
            for b in range(KERNEL):
                part = None
                for a in range(KERNEL):
                    field = wide[row + a, :, lanes].reshape(width // 8, 8, 128)
                    term = field * taps_ref[a * KERNEL + b, :, lanes][None]
                    part = term if part is None else part + term
                first = SIDE - KERNEL // 2 + b
                part = part.reshape(width, 128)[first : first + cols]
                total = part if total is None else total + part
            out_ref[row, :, lanes] = total


def forward_kernel(
    lat_count, lon_count, x_ref, edge_ref, taps_ref, out_ref, field_ref,
    wide, got_rows, got_edges, send_sem, recv_sem,
):
    radius = KERNEL // 2
    peers = rim_peers(lat_count, lon_count)
    barrier_with(peers)
    copies = send_rim(
        sender(send_sem, recv_sem), peers, radius, x_ref, edge_ref, got_rows, got_edges
    )
    fill_tile(radius, x_ref, wide)
    for copy in copies:
        copy.wait()
    fill_rim(lat_count, radius, x_ref, wide, got_rows, got_edges)

    @pl.loop(0, wide.shape[0])
    def _(row):
        field_ref[row] = wide[row].astype(jnp.bfloat16)

    conv_rows(wide, taps_ref, out_ref, 0, x_ref.shape[0])


def backward_kernel(
    lat_count, lon_count, scale, x_ref, edge_ref, taps_ref, narrow_ref, broad_ref,
    out_ref, narrow_out, broad_out,
    wide, got_rows, got_edges, n_got1, n_sum1, n_got2, n_sum2, n_got3,
    b_got1, b_sum1, b_got2, b_sum2, b_got3, send_sem, recv_sem,
):
    radius = KERNEL // 2
    rows = x_ref.shape[0]
    bands = lat_count // 2
    lat, lon = lax.axis_index("lat"), lax.axis_index("lon")
    core, band = lax.rem(lat, 2), lax.div(lat, 2)
    pair = (lat + 1 - 2 * core, lon)
    others = [lax.rem(band + k, bands) for k in range(1, bands)]
    along = [lax.rem(lon + k, lon_count) for k in range(1, lon_count)]
    peers = rim_peers(lat_count, lon_count)
    other_peers = [(2 * b + core, lon) for b in others]
    along_peers = [(lat, m) for m in along]
    barrier_with(peers + [pair] + other_peers + along_peers)
    send = sender(send_sem, recv_sem)

    def wide_sum(*terms):
        total = terms[0].astype(jnp.float32)
        for term in terms[1:]:
            total = total + term.astype(jnp.float32)
        return total

    first = [
        send(ref.at[:, 1 - core], got, pair)
        for ref, got in ((narrow_ref, n_got1), (broad_ref, b_got1))
    ]
    rim = send_rim(send, peers, radius, x_ref, edge_ref, got_rows, got_edges)
    fill_tile(radius, x_ref, wide)
    for copy, ref, got, total in zip(
        first, (narrow_ref, broad_ref), (n_got1, b_got1), (n_sum1, b_sum1)
    ):
        copy.wait()
        for b in range(bands):
            total[b] = wide_sum(ref[b, core], got[b]).astype(jnp.bfloat16)
    n_second = [
        send(n_sum1.at[:, m], n_got2.at[k], peer)
        for k, (m, peer) in enumerate(zip(along, along_peers))
    ]
    b_second = [
        send(b_sum1.at[b], b_got2.at[k], peer)
        for k, (b, peer) in enumerate(zip(others, other_peers))
    ]
    for copy in rim:
        copy.wait()
    fill_rim(lat_count, radius, x_ref, wide, got_rows, got_edges)
    conv_rows(wide, taps_ref, out_ref, 0, rows // 2)
    for copy in b_second:
        copy.wait()
    b_sum2[...] = wide_sum(b_sum1[band], *[b_got2[k] for k in range(bands - 1)]).astype(
        jnp.bfloat16
    )
    b_third = [
        send(b_sum2.at[m], b_got3.at[k], peer)
        for k, (m, peer) in enumerate(zip(along, along_peers))
    ]
    for copy in n_second:
        copy.wait()
    for b in range(bands):
        n_sum2[b] = wide_sum(
            n_sum1[b, lon], *[n_got2[k, b] for k in range(lon_count - 1)]
        ).astype(jnp.bfloat16)
    n_third = [
        send(n_sum2.at[b], n_got3.at[k], peer)
        for k, (b, peer) in enumerate(zip(others, other_peers))
    ]
    conv_rows(wide, taps_ref, out_ref, rows // 2, rows)
    for copy in n_third:
        copy.wait()
    narrow_out[...] = scale * wide_sum(n_sum2[band], *[n_got3[k] for k in range(bands - 1)])
    for copy in b_third:
        copy.wait()
    broad_out[...] = scale * wide_sum(b_sum2[lon], *[b_got3[k] for k in range(lon_count - 1)])


def edge_columns(cells):
    radius = KERNEL // 2
    sides = (cells[:, :radius], cells[:, cells.shape[1] - radius :])
    return jnp.stack([jnp.transpose(s, (1, 0, 2)) for s in sides])


def tap_rows(kernel):
    taps = kernel.astype(jnp.float32).reshape(KERNEL * KERNEL, 1, kernel.shape[2])
    return jnp.broadcast_to(taps, (KERNEL * KERNEL, 8, kernel.shape[2]))


def rim_scratch(tile):
    rows, cols, channels = tile.shape
    radius = KERNEL // 2
    return [
        pltpu.VMEM((rows + 2 * radius, cols + 2 * SIDE, channels), jnp.float32),
        pltpu.VMEM((2, radius, cols, channels), jnp.bfloat16),
        pltpu.VMEM((2, 3, radius, rows, channels), jnp.bfloat16),
    ]


VMEM_SPEC = pl.BlockSpec(memory_space=pltpu.VMEM)


def forward_conv(tile, kernel):
    rows, cols, channels = tile.shape
    radius = KERNEL // 2
    convolved, field = pl.pallas_call(
        functools.partial(forward_kernel, lax.axis_size("lat"), lax.axis_size("lon")),
        out_shape=[
            jax.ShapeDtypeStruct(tile.shape, jnp.float32),
            jax.ShapeDtypeStruct((rows + 2 * radius, cols + 2 * SIDE, channels), jnp.bfloat16),
        ],
        in_specs=[VMEM_SPEC] * 3,
        out_specs=[VMEM_SPEC] * 2,
        scratch_shapes=rim_scratch(tile)
        + [pltpu.SemaphoreType.DMA((8,)), pltpu.SemaphoreType.DMA((8,))],
        compiler_params=pltpu.CompilerParams(
            collective_id=0, has_side_effects=True, vmem_limit_bytes=24 << 20
        ),
    )(tile, edge_columns(tile), tap_rows(kernel))
    return convolved, field[:, SIDE - radius : SIDE + cols + radius]


def backward_conv(tile, kernel, narrow, broad, scale):
    lat_count, lon_count = lax.axis_size("lat"), lax.axis_size("lon")
    bands = lat_count // 2
    shares = [a.reshape((bands, 2, lon_count) + a.shape[1:]) for a in (narrow, broad)]
    n_tail, b_tail = narrow.shape[1:], broad.shape[1:]
    copies = 8 + 2 * (1 + (bands - 1) + (lon_count - 1))

    def scratch(tail, *leads):
        return [pltpu.VMEM(lead + tail, jnp.bfloat16) for lead in leads]

    return pl.pallas_call(
        functools.partial(backward_kernel, lat_count, lon_count, scale),
        out_shape=[
            jax.ShapeDtypeStruct(tile.shape, jnp.float32),
            jax.ShapeDtypeStruct(n_tail, jnp.float32),
            jax.ShapeDtypeStruct(b_tail, jnp.float32),
        ],
        in_specs=[VMEM_SPEC] * 5,
        out_specs=[VMEM_SPEC] * 3,
        scratch_shapes=rim_scratch(tile)
        + scratch(
            n_tail, (bands, lon_count), (bands, lon_count), (lon_count - 1, bands), (bands,),
            (bands - 1,),
        )
        + scratch(
            b_tail, (bands, lon_count), (bands, lon_count), (bands - 1, lon_count), (lon_count,),
            (lon_count - 1,),
        )
        + [pltpu.SemaphoreType.DMA((copies,)), pltpu.SemaphoreType.DMA((copies,))],
        compiler_params=pltpu.CompilerParams(
            collective_id=1, has_side_effects=True, vmem_limit_bytes=40 << 20
        ),
    )(tile, edge_columns(tile), tap_rows(kernel[::-1, ::-1]), *shares)


def packed_shares(grads, device_count, width):
    parts = [
        jnp.pad(
            g.astype(jnp.bfloat16).reshape(device_count, -1, g.shape[1]),
            ((0, 0), (0, 0), (0, width - g.shape[1])),
        )
        for g in grads
    ]
    rows = sum(p.shape[1] for p in parts)
    parts.append(jnp.zeros((device_count, -rows % 16, width), jnp.bfloat16))
    return jnp.concatenate(parts, axis=1)


def gelu_fn(values_in):
    return jax.nn.gelu(values_in, approximate=True)


def gelu_back(pre_act, upstream):
    return jax.vjp(gelu_fn, pre_act)[1](upstream)[0]


def kernel_terms(wide_field, grad_field, kernel_size):
    row_count = grad_field.shape[0]
    col_count = grad_field.shape[1]
    terms_list = []
    for row_off in range(kernel_size):
        for col_off in range(kernel_size):
            window = wide_field[
                row_off : row_off + row_count, col_off : col_off + col_count
            ].astype(jnp.float32)
            terms_list.append(jnp.sum(grad_field * window, axis=(0, 1)))
    return jnp.stack(terms_list).reshape(kernel_size, kernel_size, grad_field.shape[2])


def physics_forward(col_rows, column_in, column_out):
    column_pre = jnp.dot(col_rows, column_in, preferred_element_type=jnp.float32)
    inner = gelu_fn(column_pre).astype(jnp.bfloat16)
    state_full = col_rows.astype(jnp.float32) + jnp.dot(
        inner, column_out, preferred_element_type=jnp.float32
    )
    return (column_pre, inner, state_full)


def physics_backward(col_rows, column_pre, inner, target, column_in, column_out):
    inner_back = jnp.dot(target, column_out.T, preferred_element_type=jnp.float32)
    column_pre_grad = gelu_back(column_pre, inner_back).astype(jnp.bfloat16)
    column_grad = (
        target.astype(jnp.float32)
        + jnp.dot(column_pre_grad, column_in.T, preferred_element_type=jnp.float32)
    ).astype(jnp.bfloat16)
    grad_cin = jnp.dot(column_pre_grad.T, col_rows, preferred_element_type=jnp.float32)
    grad_cout = jnp.dot(inner.T, target, preferred_element_type=jnp.float32)
    return (column_grad, grad_cin, grad_cout)


def local(
    latent,
    ocean_mask,
    depth_kernel,
    expand_weight,
    reduce_weight,
    decode_weight,
    column_in,
    column_out,
    state_cot,
):
    tile_rows, tile_cols, channels = latent.shape
    cell_count = tile_rows * tile_cols
    col_width = state_cot.shape[2]
    device_count = lax.axis_size("lat") * lax.axis_size("lon")
    grad_scale = 1.0 / math.sqrt(cell_count * device_count)
    ocean = ocean_mask.astype(latent.dtype)
    masked = latent * ocean[:, :, None]
    convolved, wide_field = forward_conv(masked, depth_kernel)
    convolved = convolved.reshape(cell_count, channels)
    row_mean = jnp.mean(convolved, axis=1, keepdims=True)
    centred = convolved - row_mean
    inverse_scale = lax.rsqrt(jnp.mean(centred * centred, axis=1, keepdims=True) + EPSILON)
    unit_rows = centred * inverse_scale
    normed = unit_rows.astype(jnp.bfloat16)
    expand_pre = jnp.dot(normed, expand_weight, preferred_element_type=jnp.float32)
    hidden = gelu_fn(expand_pre).astype(jnp.bfloat16)
    masked_flat = masked.reshape(cell_count, channels)
    feature = (
        masked_flat.astype(jnp.float32)
        + jnp.dot(hidden, reduce_weight, preferred_element_type=jnp.float32)
    ).astype(jnp.bfloat16)
    column = jnp.dot(feature, decode_weight, preferred_element_type=jnp.float32).astype(
        jnp.bfloat16
    )
    ocean_flat = ocean_mask.reshape(cell_count)
    cot_flat = state_cot.reshape(cell_count, col_width)
    ocean_rows = ocean_flat.astype(jnp.float32)[:, None]
    column_pre, inner, state_full = physics_forward(column, column_in, column_out)
    state_home = (ocean_rows * state_full).astype(jnp.bfloat16)
    target = (cot_flat.astype(jnp.float32) * ocean_rows).astype(jnp.bfloat16)
    column_grad, grad_cin, grad_cout = physics_backward(
        column, column_pre, inner, target, column_in, column_out
    )
    feature_back = jnp.dot(column_grad, decode_weight.T, preferred_element_type=jnp.float32)
    feature_grad = feature_back.astype(jnp.bfloat16)
    hidden_back = jnp.dot(feature_grad, reduce_weight.T, preferred_element_type=jnp.float32)
    expand_grad = gelu_back(expand_pre, hidden_back).astype(jnp.bfloat16)
    normed_back = jnp.dot(expand_grad, expand_weight.T, preferred_element_type=jnp.float32)
    conv_grad = (
        inverse_scale
        * (
            normed_back
            - jnp.mean(normed_back, axis=1, keepdims=True)
            - unit_rows * jnp.mean(normed_back * unit_rows, axis=1, keepdims=True)
        )
    ).astype(jnp.bfloat16)
    conv_tile = conv_grad.reshape(tile_rows, tile_cols, channels)
    grad_kernel = kernel_terms(wide_field, conv_tile.astype(jnp.float32), depth_kernel.shape[0])
    grad_expand = jnp.dot(expand_grad.T, normed, preferred_element_type=jnp.float32)
    grad_reduce = jnp.dot(hidden.T, feature_grad, preferred_element_type=jnp.float32)
    grad_decode = jnp.dot(feature.T, column_grad, preferred_element_type=jnp.float32)
    kernel_rows = grad_kernel.reshape(-1, channels).T
    back_terms, narrow, broad = backward_conv(
        conv_tile,
        depth_kernel,
        packed_shares((grad_expand, grad_reduce), device_count, channels),
        packed_shares((grad_cin, grad_cout, grad_decode, kernel_rows), device_count, col_width),
        grad_scale,
    )
    grad_latent = (
        ocean_mask.astype(jnp.float32)[:, :, None]
        * (feature_back.reshape(tile_rows, tile_cols, channels) + back_terms)
    ).astype(jnp.bfloat16)
    hidden_share = grad_expand.shape[0] // device_count
    inner_share = grad_cin.shape[0] // device_count
    chan_share = channels // device_count
    tail = 2 * inner_share
    taps = depth_kernel.shape[:2]
    return (
        state_home.reshape(tile_rows, tile_cols, col_width),
        grad_latent,
        broad[tail + chan_share : tail + 2 * chan_share, : taps[0] * taps[1]]
        .T.reshape(taps + (chan_share,)),
        narrow[:hidden_share].T,
        narrow[hidden_share : 2 * hidden_share],
        broad[tail : tail + chan_share],
        broad[:inner_share].T,
        broad[inner_share:tail],
    )


def solution(mesh):
    in_specs = (
        P("lat", "lon", None),
        P("lat", "lon"),
        P(),
        P(),
        P(),
        P(),
        P(),
        P(),
        P("lat", "lon", None),
    )
    out_specs = (
        P("lat", "lon", None),
        P("lat", "lon", None),
        P(None, None, ("lat", "lon")),
        P(None, ("lat", "lon")),
        P(("lat", "lon"), None),
        P(("lat", "lon"), None),
        P(None, ("lat", "lon")),
        P(("lat", "lon"), None),
    )
    return jax.shard_map(local, mesh=mesh, in_specs=in_specs, out_specs=out_specs, check_vma=False)
```

profile of v0, /device:TPU:0, one launch (start us, length us, event | category | flops | bytes accessed | tf_op | source)
XLA Modules:
  0.0 141.5 jit_solution(7593831490832022916)
XLA Ops:
  0.6 0.8 fusion.75
  1.6 0.8 rev.3
  2.4 0.8 reshape.118
  3.2 0.8 broadcast_in_dim.32.taps_ref
  4.0 1.6 %copy_multiply_fusion = bf16[16,96,256]{2,0,1:T(8,128)(2,1)S(1)} fusion(bf16[16,96,256]{2,1,0:T(8,128)(2,1)} %param.9, bf16[16,96]{0,1:T(8,128)(2,1)S(1)} %copy.89), kind=kLoop, calls=%fused_computation.142 | loop fusion | flops 393216 | bytes 1575936 | tf_op jit(solution)/shard_map/mul | solution.py:376
  5.9 1.4 %copy.91 = f32[16,96,256]{2,1,0:T(8,128)} copy(bf16[16,96,256]{2,0,1:T(8,128)(2,1)S(1)} %copy_multiply_fusion) | data formatting | bytes 2359296 | tf_op jit(solution)/shard_map/convert_element_type | solution.py:388
  7.4 18.9 %shard_map.152 = (f32[16,96,256]{2,1,0:T(8,128)S(1)}, bf16[22,112,256]{2,1,0:T(8,128)(2,1)S(1)}) custom-call(bf16[16,96,256]{2,1,0:T(8,128)(2,1)S(1)} %copy.92.x_ref, bf16[2,3,16,256]{3,2,1,0:T(8,128)(2,1)S(1)} %pad_maximum_fusion.2.edge_ref, f32[49,8,256]{2,1,0:T(8,128)S(1)} %broadcast_in_dim.29.taps_ref), custom_call_target="tpu_custom_call" | custom-call | tf_op jit(solution)/shard_map/pallas_call | solution.py:252
  26.7 0.6 multiply_reduce_fusion.1
  27.3 1.4 fusion.68
  28.7 1.7 %bitcast_convert_fusion = f32[1536,304]{1,0:T(8,128)} fusion(bf16[16,96,304]{2,1,0:T(8,128)(2,1)S(1)} %copy-done.17), kind=kLoop, calls=%fused_computation.139 | loop fusion | flops 466944 | bytes 2801664 | tf_op jit(solution)/shard_map/convert_element_type | solution.py:399
  30.4 2.9 %copy.103 = f32[1536,304]{0,1:T(8,128)} copy(f32[1536,304]{1,0:T(8,128)} %bitcast_convert_fusion) | data formatting | bytes 3735552 | tf_op jit(solution)/shard_map/convert_element_type | solution.py:399
  33.3 1.8 %multiply_convert_fusion.2 = bf16[1536,304]{0,1:T(8,128)(2,1)S(1)} fusion(f32[1536,304]{0,1:T(8,128)} %copy.103, f32[1536]{0:T(1024)S(1)} %convert_element_type.245), kind=kLoop, calls=%fused_computation.78 | loop fusion | flops 933888 | bytes 2807808 | tf_op jit(solution)/shard_map/convert_element_type | solution.py:399
  35.2 1.0 fusion.76
  36.1 0.8 copy-done.16
  37.0 2.3 %fusion.17 = bf16[1536,256]{1,0:T(8,128)(2,1)S(1)} fusion(f32[1536,256]{1,0:T(8,128)S(1)} %bitcast.85, bf16[1024,256]{1,0:T(8,128)(2,1)S(1)} %copy-done.28, f32[1536,1024]{1,0:T(8,128)S(1)} %fusion.76), kind=kOutput, calls=%fused_computation.76 | convolution fusion | flops 820248576 | bytes 9175040 | tf_op jit(solution)/shard_map/dot_general | solution.py:389
  39.7 0.4 convolution_convert_fusion
  40.1 0.9 copy-done.10
  41.0 1.8 %fusion.77 = f32[1536,1024]{1,0:T(8,128)S(1)} fusion(bf16[1536,304]{0,1:T(8,128)(2,1)S(1)} %convolution_convert_fusion, bf16[304,1024]{1,0:T(8,128)(2,1)S(1)} %copy-done.23), kind=kOutput, calls=%fused_computation.164 | convolution fusion | flops 956301312 | bytes 7847936 | tf_op jit(solution)/shard_map/dot_general | solution.py:339
  42.9 2.6 %copy-done.6 = f32[1536,1024]{1,0:T(8,128)} copy-done((f32[1536,1024]{1,0:T(8,128)}, f32[1536,1024]{1,0:T(8,128)S(1)}, u32[]{:S(2)}) %copy-start.6) | copy-done | bytes 6291480
  45.6 3.4 %convolution_convert_fusion.1 = bf16[1024,304]{0,1:T(8,128)(2,1)} fusion(bf16[1536,304]{0,1:T(8,128)(2,1)S(1)} %multiply_convert_fusion.2, f32[1536,1024]{1,0:T(8,128)S(1)} %fusion.77), kind=kOutput, calls=%fused_computation.134 | convolution fusion | flops 970768384 | bytes 7847936 | tf_op jit(solution)/shard_map/dot_general | solution.py:355
  48.9 2.3 %copy.97 = bf16[1024,304]{1,0:T(8,128)(2,1)} copy(bf16[1024,304]{0,1:T(8,128)(2,1)} %convolution_convert_fusion.1) | data formatting | bytes 1245184 | tf_op jit(solution)/shard_map/convert_element_type | solution.py:307
  51.2 6.7 %fusion.15 = bf16[1536,304]{0,1:T(8,128)(2,1)} fusion(bf16[1024,304]{0,1:T(8,128)(2,1)S(1)} %copy-done, bf16[1536,304]{0,1:T(8,128)(2,1)} %copy-done.10, f32[1536]{0:T(1024)S(1)} %convert_element_type.245, f32[1536,1024]{1,0:T(8,128)} %copy-done.6), kind=kOutput, calls=%fused_computation.74 | convolution fusion | flops 972324864 | bytes 8787968 | tf_op jit(solution)/shard_map/dot_general | solution.py:341
  57.9 5.8 %fusion.13 = bf16[1536,1024]{1,0:T(8,128)(2,1)S(1)} fusion(f32[1536,1024]{1,0:T(8,128)S(1)} %copy-done.7, bf16[1536,304]{0,1:T(8,128)(2,1)S(1)} %copy-done.20, bf16[1024,304]{0,1:T(8,128)(2,1)S(1)} %copy-done), kind=kOutput, calls=%fused_computation.66 | convolution fusion | flops 987758592 | bytes 10993664 | tf_op jit(solution)/shard_map/dot_general | solution.py:348
  63.7 2.0 %convolution_convert_fusion.2 = bf16[1024,304]{0,1:T(8,128)(2,1)} fusion(bf16[1536,304]{0,1:T(8,128)(2,1)S(1)} %copy-done.11, bf16[1536,1024]{1,0:T(8,128)(2,1)S(1)} %fusion.13), kind=kOutput, calls=%fused_computation.135 | convolution fusion | flops 956612608 | bytes 4702208 | tf_op jit(solution)/shard_map/dot_general | solution.py:354
  65.7 1.2 fusion.16
  66.9 0.9 copy-done.18
  67.8 1.1 convolution_convert_fusion.5
  68.9 1.7 %copy.98 = bf16[256,304]{1,0:T(8,128)(2,1)} copy(bf16[256,304]{0,1:T(8,128)(2,1)} %convolution_convert_fusion.5) | data formatting | bytes 311296 | tf_op jit(solution)/shard_map/convert_element_type | solution.py:307
  70.6 2.3 %copy.96 = bf16[1024,304]{1,0:T(8,128)(2,1)} copy(bf16[1024,304]{0,1:T(8,128)(2,1)} %convolution_convert_fusion.2) | data formatting | bytes 1245184 | tf_op jit(solution)/shard_map/convert_element_type | solution.py:307
  72.9 2.3 %copy.102 = bf16[1536,304]{1,0:T(8,128)(2,1)} copy(bf16[1536,304]{0,1:T(8,128)(2,1)} %fusion.15) | data formatting | bytes 1867776
  75.2 1.9 %fusion.78 = f32[1536,256]{1,0:T(8,128)S(1)} fusion(bf16[1536,304]{0,1:T(8,128)(2,1)} %copy-done.18, bf16[256,304]{0,1:T(8,128)(2,1)} %param.14), kind=kOutput, calls=%fused_computation.165 | convolution fusion | flops 239075328 | bytes 2662400 | tf_op jit(solution)/shard_map/dot_general | solution.py:403
  77.2 6.0 %convolution_convert_fusion.3 = bf16[1024,256]{1,0:T(8,128)(2,1)S(1)} fusion(f32[1536,256]{1,0:T(8,128)S(1)} %fusion.78, f32[1536,1024]{1,0:T(8,128)} %copy-done.5), kind=kOutput, calls=%fused_computation.136 | convolution fusion | flops 820117504 | bytes 8388608 | tf_op jit(solution)/shard_map/dot_general | solution.py:419
  83.3 4.8 %fusion.6 = bf16[1536,1024]{1,0:T(8,128)(2,1)S(1)} fusion(f32[1536,1024]{1,0:T(8,128)S(1)} %bitcast.81, bf16[1024,256]{1,0:T(8,128)(2,1)S(1)} %copy-done.29, f32[1536,256]{1,0:T(8,128)S(1)} %fusion.78), kind=kOutput, calls=%fused_computation.59 | convolution fusion | flops 837156864 | bytes 11534336 | tf_op jit(solution)/shard_map/dot_general | solution.py:405
  88.1 1.0 convolution_convert_fusion.4
  89.1 1.2 fusion.71
  90.3 1.1 pad_maximum_fusion.1.narrow_ref
  91.4 1.2 multiply_convert_fusion.4
  92.6 3.3 %fusion.64 = (bf16[256]{0:T(256)(128)(2,1)S(1)}, bf16[256]{0:T(256)(128)(2,1)S(1)}, bf16[256]{0:T(256)(128)(2,1)S(1)}, bf16[256]{0:T(256)(128)(2,1)S(1)}, bf16[2...) fusion(bf16[16,96,256]{2,1,0:T(8,128)(2,1)S(1)} %bitcast.75, ...), kind=kLoop, calls=%fused_computation.125 | loop fusion | flops 15725312 | bytes 11016704 | tf_op jit(solution)/shard_map/reduce_sum | solution.py:334
  96.0 4.1 %fusion.66 = (bf16[256]{0:T(256)(128)(2,1)S(1)}, bf16[256]{0:T(256)(128)(2,1)S(1)}, bf16[256]{0:T(256)(128)(2,1)S(1)}, bf16[256]{0:T(256)(128)(2,1)S(1)}, bf16[2...) fusion(bf16[16,96,256]{2,1,0:T(8,128)(2,1)S(1)} %bitcast.76, ...), kind=kLoop, calls=%fused_computation.127 | loop fusion | flops 21622272 | bytes 14951424 | tf_op jit(solution)/shard_map/reduce_sum | solution.py:334
  100.2 4.2 %fusion.65 = (bf16[256]{0:T(256)(128)(2,1)S(1)}, bf16[256]{0:T(256)(128)(2,1)S(1)}, bf16[256]{0:T(256)(128)(2,1)S(1)}, bf16[256]{0:T(256)(128)(2,1)S(1)}, bf16[2...) fusion(bf16[16,96,256]{2,1,0:T(8,128)(2,1)S(1)} %bitcast.77, ...), kind=kLoop, calls=%fused_computation.126 | loop fusion | flops 21622272 | bytes 14951424 | tf_op jit(solution)/shard_map/reduce_sum | solution.py:334
  105.1 0.9 fusion.72
  106.2 1.3 pad_maximum_fusion.broad_ref
  107.8 29.9 %shard_map.153 = (f32[16,96,256]{2,1,0:T(8,128)S(1)}, f32[64,256]{1,0:T(8,128)S(1)}, f32[80,304]{1,0:T(8,128)S(1)}) custom-call(bf16[16,96,256]{2,1,0:T(8,128)(2,1)S(1)} %bitcast.79, bf16[2,3,16,256]{3,2,1,0:T(8,128)(2,1)S(1)} %pad_maximum_fusion.3.edge_ref, f32[49,8,256]{2,1,0:T(8,128)S(1)} %copy-done.4, bf16[2,2,8,64,256]{4,3,2,1,0:T(8,128)(2,1)S(1)} %copy-done.3, ...), custom_call_target="tpu_custom_call" | custom-call | tf_op jit(solution)/shard_map/pallas_call | solution.py:279
  137.6 1.2 multiply_convert_fusion.3
  138.8 0.6 slice.283
  139.4 0.6 fusion.73
  140.1 0.7 copy.101
  140.9 0.6 fusion.74
  (131 shorter events, 2.6 us)
Async XLA Ops:
  0.6 50.6 %copy-start = (bf16[1024,304]{0,1:T(8,128)(2,1)S(1)}, bf16[1024,304]{0,1:T(8,128)(2,1)}, u32[]{:S(2)}) copy-start(bf16[1024,304]{0,1:T(8,128)(2,1)} %param.16) | copy-start | bytes 1867780
  27.3 1.4 copy-start.17
  33.3 1.8 %copy-start.12 = (bf16[1536,256]{1,0:T(8,128)(2,1)S(1)}, bf16[1536,256]{1,0:T(8,128)(2,1)}, u32[]{:S(2)}) copy-start(bf16[1536,256]{1,0:T(8,128)(2,1)} %fusion.68) | copy-start | bytes 2359300
  33.3 1.8 %copy-start.26 = (bf16[256,1024]{1,0:T(8,128)(2,1)S(1)}, bf16[256,1024]{1,0:T(8,128)(2,1)}, u32[]{:S(2)}) copy-start(bf16[256,1024]{1,0:T(8,128)(2,1)} %param.12) | copy-start | bytes 1572868
  35.1 7.7 %copy-start.19 = (bf16[1536,304]{0,1:T(8,128)(2,1)}, bf16[1536,304]{0,1:T(8,128)(2,1)S(1)}, u32[]{:S(2)}) copy-start(bf16[1536,304]{0,1:T(8,128)(2,1)S(1)} %multiply_convert_fusion.2) | copy-start | bytes 2801668
  35.1 1.7 %copy-start.16 = (f32[16,96,256]{2,1,0:T(8,128)S(1)}, f32[16,96,256]{2,1,0:T(8,128)}, u32[]{:S(2)}) copy-start(f32[16,96,256]{2,1,0:T(8,128)} %copy.91) | copy-start | bytes 4718596
  35.1 1.9 %copy-start.28 = (bf16[1024,256]{1,0:T(8,128)(2,1)S(1)}, bf16[1024,256]{1,0:T(8,128)(2,1)}, u32[]{:S(2)}) copy-start(bf16[1024,256]{1,0:T(8,128)(2,1)} %param.13) | copy-start | bytes 1572868
  37.0 2.7 %copy-start.5 = (f32[1536,1024]{1,0:T(8,128)}, f32[1536,1024]{1,0:T(8,128)S(1)}, u32[]{:S(2)}) copy-start(f32[1536,1024]{1,0:T(8,128)S(1)} %fusion.76) | copy-start | bytes 18874372
  37.0 2.7 %copy-start.25 = (bf16[256,304]{0,1:T(8,128)(2,1)S(1)}, bf16[256,304]{0,1:T(8,128)(2,1)}, u32[]{:S(2)}) copy-start(bf16[256,304]{0,1:T(8,128)(2,1)} %param.14) | copy-start | bytes 466948
  39.7 3.2 %copy-start.21 = (bf16[1536,256]{1,0:T(8,128)(2,1)}, bf16[1536,256]{1,0:T(8,128)(2,1)S(1)}, u32[]{:S(2)}) copy-start(bf16[1536,256]{1,0:T(8,128)(2,1)S(1)} %fusion.17) | copy-start | bytes 2359300
  39.7 1.4 copy-start.23
  40.1 0.9 copy-start.10
  42.9 2.7 %copy-start.6 = (f32[1536,1024]{1,0:T(8,128)}, f32[1536,1024]{1,0:T(8,128)S(1)}, u32[]{:S(2)}) copy-start(f32[1536,1024]{1,0:T(8,128)S(1)} %fusion.77) | copy-start | bytes 18874372
  51.2 6.7 %copy-start.7 = (f32[1536,1024]{1,0:T(8,128)S(1)}, f32[1536,1024]{1,0:T(8,128)}, u32[]{:S(2)}) copy-start(f32[1536,1024]{1,0:T(8,128)} %copy-done.6) | copy-start | bytes 18874372
  51.2 6.7 %copy-start.20 = (bf16[1536,304]{0,1:T(8,128)(2,1)S(1)}, bf16[1536,304]{0,1:T(8,128)(2,1)}, u32[]{:S(2)}) copy-start(bf16[1536,304]{0,1:T(8,128)(2,1)} %copy-done.19) | copy-start | bytes 2801668
  57.9 5.8 %copy-start.11 = (bf16[1536,304]{0,1:T(8,128)(2,1)S(1)}, bf16[1536,304]{0,1:T(8,128)(2,1)}, u32[]{:S(2)}) copy-start(bf16[1536,304]{0,1:T(8,128)(2,1)} %copy-done.10) | copy-start | bytes 2801668
  63.7 2.0 %copy-start.24 = (bf16[304,1024]{1,0:T(8,128)(2,1)S(1)}, bf16[304,1024]{1,0:T(8,128)(2,1)}, u32[]{:S(2)}) copy-start(bf16[304,1024]{1,0:T(8,128)(2,1)} %param.15) | copy-start | bytes 1867780
  65.7 2.1 %copy-start.22 = (bf16[1536,256]{1,0:T(8,128)(2,1)S(1)}, bf16[1536,256]{1,0:T(8,128)(2,1)}, u32[]{:S(2)}) copy-start(bf16[1536,256]{1,0:T(8,128)(2,1)} %copy-done.21) | copy-start | bytes 2359300
  66.9 0.9 copy-start.18
  75.2 8.0 %slice-start = ((s8[6291456]{0:T(1024)(128)(4,1)}), s8[4194304]{0:T(1024)(128)(4,1)S(1)}, s32[]{:S(2)}) async-start(s8[6291456]{0:T(1024)(128)(4,1)} %bitcast.80), calls=%async_computation | async-start | bytes 8388608
  77.2 6.0 %copy-start.8 = (f32[1536,256]{1,0:T(8,128)}, f32[1536,256]{1,0:T(8,128)S(1)}, u32[]{:S(2)}) copy-start(f32[1536,256]{1,0:T(8,128)S(1)} %fusion.78) | copy-start | bytes 4718596
  77.2 6.0 %slice-start.1 = ((s8[6291456]{0:T(1024)(128)(4,1)}), s8[2097152]{0:T(1024)(128)(4,1)S(1)}, s32[]{:S(2)}) async-start(s8[6291456]{0:T(1024)(128)(4,1)} %bitcast.80), calls=%async_computation.1 | async-start | bytes 4194304
  77.2 6.0 %copy-start.29 = (bf16[1024,256]{1,0:T(8,128)(2,1)S(1)}, bf16[1024,256]{1,0:T(8,128)(2,1)}, u32[]{:S(2)}) copy-start(bf16[1024,256]{1,0:T(8,128)(2,1)} %param.13) | copy-start | bytes 1572868
  83.3 4.8 %copy-start.13 = (bf16[1536,256]{1,0:T(8,128)(2,1)S(1)}, bf16[1536,256]{1,0:T(8,128)(2,1)}, u32[]{:S(2)}) copy-start(bf16[1536,256]{1,0:T(8,128)(2,1)} %fusion.68) | copy-start | bytes 2359300
  88.1 1.0 copy-start.27
  92.6 7.6 %copy-start.1 = (bf16[1536,256]{1,0:T(8,128)(2,1)}, bf16[1536,256]{1,0:T(8,128)(2,1)S(1)}, u32[]{:S(2)}) copy-start(bf16[1536,256]{1,0:T(8,128)(2,1)S(1)} %multiply_convert_fusion.4) | copy-start | bytes 2359300
  100.2 5.9 %copy-start.14 = (bf16[1024,304]{1,0:T(8,128)(2,1)S(1)}, bf16[1024,304]{1,0:T(8,128)(2,1)}, u32[]{:S(2)}) copy-start(bf16[1024,304]{1,0:T(8,128)(2,1)} %copy.97) | copy-start | bytes 1867780
  100.2 5.9 %copy-start.15 = (bf16[1024,304]{1,0:T(8,128)(2,1)S(1)}, bf16[1024,304]{1,0:T(8,128)(2,1)}, u32[]{:S(2)}) copy-start(bf16[1024,304]{1,0:T(8,128)(2,1)} %copy.96) | copy-start | bytes 1867780
  106.1 1.3 copy-start.2
  106.1 1.6 %copy-start.3 = (bf16[2,2,8,64,256]{4,3,2,1,0:T(8,128)(2,1)S(1)}, bf16[2,2,8,64,256]{4,3,2,1,0:T(8,128)(2,1)}, u32[]{:S(2)}) copy-start(bf16[2,2,8,64,256]{4,3,2,1,0:T(8,128)(2,1)} %pad_maximum_fusion.1.narrow_ref) | copy-start | bytes 3145732
  106.1 1.6 %copy-start.4 = (f32[49,8,256]{2,1,0:T(8,128)S(1)}, f32[49,8,256]{2,1,0:T(8,128)}, u32[]{:S(2)}) copy-start(f32[49,8,256]{2,1,0:T(8,128)} %broadcast_in_dim.32.taps_ref) | copy-start | bytes 1204228
  107.8 29.9 %copy-start.9 = (f32[1536,256]{1,0:T(8,128)S(1)}, f32[1536,256]{1,0:T(8,128)}, u32[]{:S(2)}) copy-start(f32[1536,256]{1,0:T(8,128)} %copy-done.8) | copy-start | bytes 4718596
where the time goes:
time: 142 us; the launch traced here: 141 us
  Pallas kernels  48.7 us (34%)
  matrix products  40.6 us (29%)
  local copies, waits for them, and re-layouts  26.3 us (19%)
  other arithmetic  24.5 us (17%)
  between operations  1.48 us (1%)
    pallas_call x1, Pallas kernels, backward_conv(): pl.pallas_call(functools.partial(backward_kernel, lat_count, lon_count, s...  29.9 us
    pallas_call x1, Pallas kernels, forward_conv(): pl.pallas_call(functools.partial(forward_kernel, lax.axis_size('lat'), la...  18.9 us
    reduce_sum x3, other arithmetic, kernel_terms(): terms_list.append(jnp.sum(grad_field * window, axis=(0, 1)))  11.6 us
    unnamed x68, local copies, waits for them, and re-layouts  9.25 us
    dot_general x1, matrix products, physics_forward(): jnp.dot(inner, column_out, preferred_element_type=jnp.float32)  6.7 us
    convert_element_type x4, local copies, waits for them, and re-layouts, packed_shares(): g.astype(jnp.bfloat16).reshape(device_count, -1, g.shape[1])  6.41 us
    dot_general x1, matrix products, local(): jnp.dot(hidden.T, feature_grad, preferred_element_type=jnp.float32)  5.99 us
    dot_general x1, matrix products, physics_backward(): jnp.dot(target, column_out.T, preferred_element_type=jnp.float32)  5.77 us

commit v1 on v0

--- a/solution.py
+++ b/solution.py
@@ -319,7 +319,12 @@
 
 
 def gelu_back(pre_act, upstream):
-    return jax.vjp(gelu_fn, pre_act)[1](upstream)[0]
+    rate = math.sqrt(2.0 / math.pi)
+    square = pre_act * pre_act
+    bend = (rate * 0.044715) * square
+    t = jnp.tanh(pre_act * (rate + bend))
+    slope = (0.5 * rate) + 1.5 * bend
+    return upstream * ((0.5 + 0.5 * t) + (pre_act * slope) * (1.0 - t * t))
 
 
 def kernel_terms(wide_field, grad_field, kernel_size):
@@ -346,7 +351,9 @@
 
 def physics_backward(col_rows, column_pre, inner, target, column_in, column_out):
     inner_back = jnp.dot(target, column_out.T, preferred_element_type=jnp.float32)
-    column_pre_grad = gelu_back(column_pre, inner_back).astype(jnp.bfloat16)
+    column_pre_grad = lax.optimization_barrier(
+        gelu_back(column_pre, inner_back).astype(jnp.bfloat16)
+    )
     column_grad = (
         target.astype(jnp.float32)
         + jnp.dot(column_pre_grad, column_in.T, preferred_element_type=jnp.float32)
@@ -396,14 +403,16 @@
     ocean_rows = ocean_flat.astype(jnp.float32)[:, None]
     column_pre, inner, state_full = physics_forward(column, column_in, column_out)
     state_home = (ocean_rows * state_full).astype(jnp.bfloat16)
-    target = (cot_flat.astype(jnp.float32) * ocean_rows).astype(jnp.bfloat16)
+    target = cot_flat * ocean_flat.astype(jnp.bfloat16)[:, None]
     column_grad, grad_cin, grad_cout = physics_backward(
         column, column_pre, inner, target, column_in, column_out
     )
     feature_back = jnp.dot(column_grad, decode_weight.T, preferred_element_type=jnp.float32)
     feature_grad = feature_back.astype(jnp.bfloat16)
     hidden_back = jnp.dot(feature_grad, reduce_weight.T, preferred_element_type=jnp.float32)
-    expand_grad = gelu_back(expand_pre, hidden_back).astype(jnp.bfloat16)
+    expand_grad = lax.optimization_barrier(
+        gelu_back(expand_pre, hidden_back).astype(jnp.bfloat16)
+    )
     normed_back = jnp.dot(expand_grad, expand_weight.T, preferred_element_type=jnp.float32)
     conv_grad = (
         inverse_scale

time: 142 us -> 138 us (0.972)
  other arithmetic: 24.5 us -> 20.1 us
  local copies, waits for them, and re-layouts: 26.3 us -> 29.1 us
  matrix products: 40.6 us -> 38.3 us
    convert_element_type x2 -> x0, other arithmetic: 3.44 us -> none  [local(): target = (cot_flat.astype(jnp.float32) * ocean_rows).astype(jnp.bfloat16)]
    convert_element_type x1, local copies, waits for them, and re-layouts: 2.92 us -> 0.09 us  [local(): target = cot_flat * ocean_flat.astype(jnp.bfloat16)[:, None]]
    unnamed x68 -> x72, local copies, waits for them, and re-layouts: 9.25 us -> 11.9 us
where the time goes in v1:
time: 138 us
  Pallas kernels  48.7 us (35%)
  matrix products  38.3 us (28%)
  local copies, waits for them, and re-layouts  29.1 us (21%)
  other arithmetic  20.1 us (15%)
  between operations  1.47 us (1%)
    pallas_call x1, Pallas kernels, backward_conv(): pl.pallas_call(functools.partial(backward_kernel, lat_count, lon_count, s...  29.9 us
    pallas_call x1, Pallas kernels, forward_conv(): pl.pallas_call(functools.partial(forward_kernel, lax.axis_size('lat'), la...  18.9 us
    unnamed x72, local copies, waits for them, and re-layouts  11.9 us
    reduce_sum x3, other arithmetic, kernel_terms(): terms_list.append(jnp.sum(grad_field * window, axis=(0, 1)))  11.6 us
    dot_general x1, matrix products, physics_forward(): jnp.dot(inner, column_out, preferred_element_type=jnp.float32)  6.7 us
    convert_element_type x4, local copies, waits for them, and re-layouts, packed_shares(): g.astype(jnp.bfloat16).reshape(device_count, -1, g.shape[1])  6.41 us
    dot_general x1, matrix products, local(): jnp.dot(hidden.T, feature_grad, preferred_element_type=jnp.float32)  6 us
    dot_general x1, matrix products, physics_backward(): jnp.dot(target, column_out.T, preferred_element_type=jnp.float32)  4.61 us

profile of v1, /device:TPU:0, one launch (start us, length us, event | category | flops | bytes accessed | tf_op | source)
XLA Modules:
  0.0 137.6 jit_solution(12763912236805416848)
XLA Ops:
  0.6 0.8 fusion.103
  1.7 0.8 rev.3
  2.5 0.8 reshape.125
  3.3 0.8 broadcast_in_dim.30.taps_ref
  4.1 0.8 broadcast_in_dim.33.taps_ref
  4.9 1.6 %copy_multiply_fusion = bf16[16,96,256]{2,0,1:T(8,128)(2,1)S(1)} fusion(bf16[16,96,256]{2,1,0:T(8,128)(2,1)} %param.9, bf16[16,96]{0,1:T(8,128)(2,1)S(1)} %copy.89), kind=kLoop, calls=%fused_computation.160 | loop fusion | flops 393216 | bytes 1575936 | tf_op jit(solution)/shard_map/mul | solution.py:383
  6.5 1.1 copy.92.x_ref
  7.6 1.4 %copy.91 = f32[16,96,256]{2,1,0:T(8,128)} copy(bf16[16,96,256]{2,0,1:T(8,128)(2,1)S(1)} %copy_multiply_fusion) | data formatting | bytes 2359296 | tf_op jit(solution)/shard_map/convert_element_type | solution.py:395
  9.1 1.4 %copy.103 = bf16[1536,304]{0,1:T(8,128)(2,1)} copy(bf16[1536,304]{1,0:T(8,128)(2,1)S(1)} %bitcast.82) | data formatting | bytes 1867776 | tf_op jit(solution)/shard_map/reshape | solution.py:402
  10.5 1.1 copy-done.4
  11.6 1.0 copy-done.6
  12.6 18.9 %shard_map.152 = (f32[16,96,256]{2,1,0:T(8,128)S(1)}, bf16[22,112,256]{2,1,0:T(8,128)(2,1)S(1)}) custom-call(bf16[16,96,256]{2,1,0:T(8,128)(2,1)S(1)} %copy-done.4, bf16[2,3,16,256]{3,2,1,0:T(8,128)(2,1)S(1)} %pad_maximum_fusion.2.edge_ref, f32[49,8,256]{2,1,0:T(8,128)S(1)} %copy-done.6), custom_call_target="tpu_custom_call" | custom-call | tf_op jit(solution)/shard_map/pallas_call | solution.py:252
  31.9 0.6 multiply_reduce_fusion.1
  33.1 0.9 copy-done.14
  34.0 1.0 fusion.104
  35.5 2.3 %fusion.37 = bf16[1536,256]{1,0:T(8,128)(2,1)S(1)} fusion(f32[1536,256]{1,0:T(8,128)S(1)} %bitcast.81, bf16[1024,256]{1,0:T(8,128)(2,1)S(1)} %copy-done.30, f32[1536,1024]{1,0:T(8,128)S(1)} %fusion.104), kind=kOutput, calls=%fused_computation.96 | convolution fusion | flops 820248576 | bytes 9175040 | tf_op jit(solution)/shard_map/dot_general | solution.py:396
  38.6 0.9 copy-done.12
  39.5 1.8 %fusion.105 = f32[1536,1024]{1,0:T(8,128)S(1)} fusion(bf16[1536,304]{0,1:T(8,128)(2,1)S(1)} %convolution_convert_fusion, bf16[304,1024]{1,0:T(8,128)(2,1)S(1)} %copy-done.25), kind=kOutput, calls=%fused_computation.186 | convolution fusion | flops 956301312 | bytes 7847936 | tf_op jit(solution)/shard_map/dot_general | solution.py:344
  41.4 2.6 %copy-done.8 = f32[1536,1024]{1,0:T(8,128)} copy-done((f32[1536,1024]{1,0:T(8,128)}, f32[1536,1024]{1,0:T(8,128)S(1)}, u32[]{:S(2)}) %copy-start.8) | copy-done | bytes 6291480
  44.0 3.4 %convolution_convert_fusion.1 = bf16[1024,304]{0,1:T(8,128)(2,1)} fusion(bf16[1536,304]{0,1:T(8,128)(2,1)S(1)} %copy-done.21, bf16[1536]{0:T(1024)(128)(2,1)S(1)} %convert_element_type.255, f32[1536,1024]{1,0:T(8,128)S(1)} %fusion.105), kind=kOutput, calls=%fused_computation.153 | convolution fusion | flops 971235328 | bytes 7851008 | tf_op jit(solution)/shard_map/dot_general | solution.py:362
  47.4 2.3 %copy.97 = bf16[1024,304]{1,0:T(8,128)(2,1)} copy(bf16[1024,304]{0,1:T(8,128)(2,1)} %convolution_convert_fusion.1) | data formatting | bytes 1245184 | tf_op jit(solution)/shard_map/convert_element_type | solution.py:307
  49.7 6.7 %fusion.35 = bf16[1536,304]{0,1:T(8,128)(2,1)} fusion(bf16[1024,304]{0,1:T(8,128)(2,1)S(1)} %copy-done, bf16[1536,304]{0,1:T(8,128)(2,1)} %copy-done.12, f32[1536]{0:T(1024)S(1)} %convert_element_type.244, f32[1536,1024]{1,0:T(8,128)} %copy-done.8), kind=kOutput, calls=%fused_computation.94 | convolution fusion | flops 972324864 | bytes 8787968 | tf_op jit(solution)/shard_map/dot_general | solution.py:346
  56.4 4.6 %fusion.33 = bf16[1536,1024]{1,0:T(8,128)(2,1)S(1)} fusion(f32[1536,1024]{1,0:T(8,128)S(1)} %copy-done.9, bf16[1024,304]{0,1:T(8,128)(2,1)S(1)} %copy-done, bf16[1536,304]{0,1:T(8,128)(2,1)S(1)} %copy-done.22, bf16[1536]{0:T(1024)(128)(2,1)S(1)} %convert_element_type.255), kind=kOutput, calls=%fused_computation.88 | convolution fusion | flops 980361216 | bytes 10996736 | tf_op jit(solution)/shard_map/dot_general | solution.py:353
  61.0 2.0 %convolution_convert_fusion.2 = bf16[1024,304]{0,1:T(8,128)(2,1)} fusion(bf16[1536,304]{0,1:T(8,128)(2,1)S(1)} %copy-done.13, bf16[1536,1024]{1,0:T(8,128)(2,1)S(1)} %fusion.33), kind=kOutput, calls=%fused_computation.154 | convolution fusion | flops 956612608 | bytes 4702208 | tf_op jit(solution)/shard_map/dot_general | solution.py:361
  63.0 1.2 fusion.36
  64.2 0.9 copy-done.20
  65.1 1.1 convolution_convert_fusion.5
  66.2 1.7 %copy.98 = bf16[256,304]{1,0:T(8,128)(2,1)} copy(bf16[256,304]{0,1:T(8,128)(2,1)} %convolution_convert_fusion.5) | data formatting | bytes 311296 | tf_op jit(solution)/shard_map/convert_element_type | solution.py:307
  67.9 2.3 %copy.96 = bf16[1024,304]{1,0:T(8,128)(2,1)} copy(bf16[1024,304]{0,1:T(8,128)(2,1)} %convolution_convert_fusion.2) | data formatting | bytes 1245184 | tf_op jit(solution)/shard_map/convert_element_type | solution.py:307
  70.2 2.3 %copy.102 = bf16[1536,304]{1,0:T(8,128)(2,1)} copy(bf16[1536,304]{0,1:T(8,128)(2,1)} %fusion.35) | data formatting | bytes 1867776
  72.5 1.9 %fusion.106 = f32[1536,256]{1,0:T(8,128)S(1)} fusion(bf16[1536,304]{0,1:T(8,128)(2,1)} %copy-done.20, bf16[256,304]{0,1:T(8,128)(2,1)} %param.14), kind=kOutput, calls=%fused_computation.187 | convolution fusion | flops 239075328 | bytes 2662400 | tf_op jit(solution)/shard_map/dot_general | solution.py:410
  74.5 6.0 %convolution_convert_fusion.3 = bf16[1024,256]{1,0:T(8,128)(2,1)S(1)} fusion(f32[1536,256]{1,0:T(8,128)S(1)} %fusion.106, f32[1536,1024]{1,0:T(8,128)} %copy-done.7), kind=kOutput, calls=%fused_computation.155 | convolution fusion | flops 820117504 | bytes 8388608 | tf_op jit(solution)/shard_map/dot_general | solution.py:428
  80.6 3.6 %fusion.16 = bf16[1536,1024]{1,0:T(8,128)(2,1)S(1)} fusion(f32[1536,1024]{1,0:T(8,128)S(1)} %bitcast.77, bf16[1024,256]{1,0:T(8,128)(2,1)S(1)} %copy-done.31, f32[1536,256]{1,0:T(8,128)S(1)} %fusion.106), kind=kOutput, calls=%fused_computation.71 | convolution fusion | flops 829292544 | bytes 11534336 | tf_op jit(solution)/shard_map/dot_general | solution.py:412
  84.2 1.0 convolution_convert_fusion.4
  85.2 1.3 fusion.99
  86.5 1.1 pad_maximum_fusion.1.narrow_ref
  87.5 1.2 multiply_convert_fusion.1
  88.7 3.1 %fusion.84 = (bf16[256]{0:T(256)(128)(2,1)S(1)}, bf16[256]{0:T(256)(128)(2,1)S(1)}, bf16[256]{0:T(256)(128)(2,1)S(1)}, bf16[256]{0:T(256)(128)(2,1)S(1)}, bf16[2...) fusion(bf16[16,96,256]{2,1,0:T(8,128)(2,1)S(1)} %bitcast.71, ...), kind=kLoop, calls=%fused_computation.144 | loop fusion | flops 15725312 | bytes 11016704 | tf_op jit(solution)/shard_map/reduce_sum | solution.py:339
  91.9 4.4 %fusion.86 = (bf16[256]{0:T(256)(128)(2,1)S(1)}, bf16[256]{0:T(256)(128)(2,1)S(1)}, bf16[256]{0:T(256)(128)(2,1)S(1)}, bf16[256]{0:T(256)(128)(2,1)S(1)}, bf16[2...) fusion(bf16[16,96,256]{2,1,0:T(8,128)(2,1)S(1)} %bitcast.72, ...), kind=kLoop, calls=%fused_computation.146 | loop fusion | flops 21622272 | bytes 14951424 | tf_op jit(solution)/shard_map/reduce_sum | solution.py:339
  96.3 4.2 %fusion.85 = (bf16[256]{0:T(256)(128)(2,1)S(1)}, bf16[256]{0:T(256)(128)(2,1)S(1)}, bf16[256]{0:T(256)(128)(2,1)S(1)}, bf16[256]{0:T(256)(128)(2,1)S(1)}, bf16[2...) fusion(bf16[16,96,256]{2,1,0:T(8,128)(2,1)S(1)} %bitcast.73, ...), kind=kLoop, calls=%fused_computation.145 | loop fusion | flops 21622272 | bytes 14951424 | tf_op jit(solution)/shard_map/reduce_sum | solution.py:339
  101.2 0.9 fusion.100
  102.3 1.3 pad_maximum_fusion.broad_ref
  103.9 29.9 %shard_map.153 = (f32[16,96,256]{2,1,0:T(8,128)S(1)}, f32[64,256]{1,0:T(8,128)S(1)}, f32[80,304]{1,0:T(8,128)S(1)}) custom-call(bf16[16,96,256]{2,1,0:T(8,128)(2,1)S(1)} %bitcast.75, bf16[2,3,16,256]{3,2,1,0:T(8,128)(2,1)S(1)} %pad_maximum_fusion.3.edge_ref, f32[49,8,256]{2,1,0:T(8,128)S(1)} %copy-done.5, bf16[2,2,8,64,256]{4,3,2,1,0:T(8,128)(2,1)S(1)} %copy-done.3, ...), custom_call_target="tpu_custom_call" | custom-call | tf_op jit(solution)/shard_map/pallas_call | solution.py:279
  133.8 1.2 multiply_convert_fusion
  134.9 0.6 slice.283
  135.5 0.6 fusion.101
  136.3 0.7 copy.101
  137.0 0.6 fusion.102
  (134 shorter events, 3.7 us)
Async XLA Ops:
  0.6 49.0 %copy-start = (bf16[1024,304]{0,1:T(8,128)(2,1)S(1)}, bf16[1024,304]{0,1:T(8,128)(2,1)}, u32[]{:S(2)}) copy-start(bf16[1024,304]{0,1:T(8,128)(2,1)} %param.16) | copy-start | bytes 1867780
  6.5 2.5 %copy-start.19 = (bf16[16,96,304]{2,1,0:T(8,128)(2,1)S(1)}, bf16[16,96,304]{2,1,0:T(8,128)(2,1)}, u32[]{:S(2)}) copy-start(bf16[16,96,304]{2,1,0:T(8,128)(2,1)} %param.17) | copy-start | bytes 2801668
  10.5 1.1 copy-start.4
  11.6 1.0 copy-start.6
  32.6 1.4 copy-start.28
  33.1 0.9 copy-start.14
  33.9 1.4 %copy-start.18 = (f32[16,96,256]{2,1,0:T(8,128)S(1)}, f32[16,96,256]{2,1,0:T(8,128)}, u32[]{:S(2)}) copy-start(f32[16,96,256]{2,1,0:T(8,128)} %copy.91) | copy-start | bytes 4718596
  34.0 1.5 %copy-start.30 = (bf16[1024,256]{1,0:T(8,128)(2,1)S(1)}, bf16[1024,256]{1,0:T(8,128)(2,1)}, u32[]{:S(2)}) copy-start(bf16[1024,256]{1,0:T(8,128)(2,1)} %param.13) | copy-start | bytes 1572868
  35.5 2.7 %copy-start.7 = (f32[1536,1024]{1,0:T(8,128)}, f32[1536,1024]{1,0:T(8,128)S(1)}, u32[]{:S(2)}) copy-start(f32[1536,1024]{1,0:T(8,128)S(1)} %fusion.104) | copy-start | bytes 18874372
  35.5 2.7 %copy-start.27 = (bf16[256,304]{0,1:T(8,128)(2,1)S(1)}, bf16[256,304]{0,1:T(8,128)(2,1)}, u32[]{:S(2)}) copy-start(bf16[256,304]{0,1:T(8,128)(2,1)} %param.14) | copy-start | bytes 466948
  38.1 3.2 %copy-start.23 = (bf16[1536,256]{1,0:T(8,128)(2,1)}, bf16[1536,256]{1,0:T(8,128)(2,1)S(1)}, u32[]{:S(2)}) copy-start(bf16[1536,256]{1,0:T(8,128)(2,1)S(1)} %fusion.37) | copy-start | bytes 2359300
  38.1 1.4 %copy-start.25 = (bf16[304,1024]{1,0:T(8,128)(2,1)S(1)}, bf16[304,1024]{1,0:T(8,128)(2,1)}, u32[]{:S(2)}) copy-start(bf16[304,1024]{1,0:T(8,128)(2,1)} %param.15) | copy-start | bytes 1867780
  38.6 0.9 copy-start.12
  39.5 4.5 %copy-start.21 = (bf16[1536,304]{0,1:T(8,128)(2,1)S(1)}, bf16[1536,304]{0,1:T(8,128)(2,1)}, u32[]{:S(2)}) copy-start(bf16[1536,304]{0,1:T(8,128)(2,1)} %copy.103) | copy-start | bytes 2801668
  41.4 2.7 %copy-start.8 = (f32[1536,1024]{1,0:T(8,128)}, f32[1536,1024]{1,0:T(8,128)S(1)}, u32[]{:S(2)}) copy-start(f32[1536,1024]{1,0:T(8,128)S(1)} %fusion.105) | copy-start | bytes 18874372
  49.7 6.7 %copy-start.9 = (f32[1536,1024]{1,0:T(8,128)S(1)}, f32[1536,1024]{1,0:T(8,128)}, u32[]{:S(2)}) copy-start(f32[1536,1024]{1,0:T(8,128)} %copy-done.8) | copy-start | bytes 18874372
  49.7 6.7 %copy-start.22 = (bf16[1536,304]{0,1:T(8,128)(2,1)S(1)}, bf16[1536,304]{0,1:T(8,128)(2,1)}, u32[]{:S(2)}) copy-start(bf16[1536,304]{0,1:T(8,128)(2,1)} %copy.103) | copy-start | bytes 2801668
  56.4 4.6 %copy-start.13 = (bf16[1536,304]{0,1:T(8,128)(2,1)S(1)}, bf16[1536,304]{0,1:T(8,128)(2,1)}, u32[]{:S(2)}) copy-start(bf16[1536,304]{0,1:T(8,128)(2,1)} %copy-done.12) | copy-start | bytes 2801668
  61.0 2.0 %copy-start.26 = (bf16[304,1024]{1,0:T(8,128)(2,1)S(1)}, bf16[304,1024]{1,0:T(8,128)(2,1)}, u32[]{:S(2)}) copy-start(bf16[304,1024]{1,0:T(8,128)(2,1)} %param.15) | copy-start | bytes 1867780
  63.0 2.1 %copy-start.24 = (bf16[1536,256]{1,0:T(8,128)(2,1)S(1)}, bf16[1536,256]{1,0:T(8,128)(2,1)}, u32[]{:S(2)}) copy-start(bf16[1536,256]{1,0:T(8,128)(2,1)} %copy-done.23) | copy-start | bytes 2359300
  64.1 0.9 copy-start.20
  72.5 8.0 %slice-start = ((s8[6291456]{0:T(1024)(128)(4,1)}), s8[4194304]{0:T(1024)(128)(4,1)S(1)}, s32[]{:S(2)}) async-start(s8[6291456]{0:T(1024)(128)(4,1)} %bitcast.76), calls=%async_computation | async-start | bytes 8388608
  74.5 6.0 %copy-start.10 = (f32[1536,256]{1,0:T(8,128)}, f32[1536,256]{1,0:T(8,128)S(1)}, u32[]{:S(2)}) copy-start(f32[1536,256]{1,0:T(8,128)S(1)} %fusion.106) | copy-start | bytes 4718596
  74.5 6.1 %slice-start.1 = ((s8[6291456]{0:T(1024)(128)(4,1)}), s8[2097152]{0:T(1024)(128)(4,1)S(1)}, s32[]{:S(2)}) async-start(s8[6291456]{0:T(1024)(128)(4,1)} %bitcast.76), calls=%async_computation.1 | async-start | bytes 4194304
  74.5 6.1 %copy-start.31 = (bf16[1024,256]{1,0:T(8,128)(2,1)S(1)}, bf16[1024,256]{1,0:T(8,128)(2,1)}, u32[]{:S(2)}) copy-start(bf16[1024,256]{1,0:T(8,128)(2,1)} %param.13) | copy-start | bytes 1572868
  80.6 3.6 %copy-start.15 = (bf16[1536,256]{1,0:T(8,128)(2,1)S(1)}, bf16[1536,256]{1,0:T(8,128)(2,1)}, u32[]{:S(2)}) copy-start(bf16[1536,256]{1,0:T(8,128)(2,1)} %copy-done.14) | copy-start | bytes 2359300
  84.1 1.0 copy-start.29
  88.7 7.6 %copy-start.1 = (bf16[1536,256]{1,0:T(8,128)(2,1)}, bf16[1536,256]{1,0:T(8,128)(2,1)S(1)}, u32[]{:S(2)}) copy-start(bf16[1536,256]{1,0:T(8,128)(2,1)S(1)} %multiply_convert_fusion.1) | copy-start | bytes 2359300
  96.3 5.9 %copy-start.16 = (bf16[1024,304]{1,0:T(8,128)(2,1)S(1)}, bf16[1024,304]{1,0:T(8,128)(2,1)}, u32[]{:S(2)}) copy-start(bf16[1024,304]{1,0:T(8,128)(2,1)} %copy.97) | copy-start | bytes 1867780
  96.3 5.9 %copy-start.17 = (bf16[1024,304]{1,0:T(8,128)(2,1)S(1)}, bf16[1024,304]{1,0:T(8,128)(2,1)}, u32[]{:S(2)}) copy-start(bf16[1024,304]{1,0:T(8,128)(2,1)} %copy.96) | copy-start | bytes 1867780
  102.2 1.3 copy-start.2
  102.3 1.6 %copy-start.3 = (bf16[2,2,8,64,256]{4,3,2,1,0:T(8,128)(2,1)S(1)}, bf16[2,2,8,64,256]{4,3,2,1,0:T(8,128)(2,1)}, u32[]{:S(2)}) copy-start(bf16[2,2,8,64,256]{4,3,2,1,0:T(8,128)(2,1)} %pad_maximum_fusion.1.narrow_ref) | copy-start | bytes 3145732
  102.3 1.6 %copy-start.5 = (f32[49,8,256]{2,1,0:T(8,128)S(1)}, f32[49,8,256]{2,1,0:T(8,128)}, u32[]{:S(2)}) copy-start(f32[49,8,256]{2,1,0:T(8,128)} %broadcast_in_dim.33.taps_ref) | copy-start | bytes 1204228
  103.9 29.9 %copy-start.11 = (f32[1536,256]{1,0:T(8,128)S(1)}, f32[1536,256]{1,0:T(8,128)}, u32[]{:S(2)}) copy-start(f32[1536,256]{1,0:T(8,128)} %copy-done.10) | copy-start | bytes 4718596
